TPU v7x, 32 devices: a whole 2x2x4 slice. The times are simulated.
32 devices in a mesh: parts: 2 (over x), ctx: 16 (over z, y, core).
Axes of the slice: x: 2, y: 2, z: 4, core: 2. Of those that a mesh axis runs over, the one named last changes fastest.
Arguments:
- hidden_states: bfloat16 [8192, 8192], P(('parts', 'ctx')), parts along dimension 0, may hold values from -6 to 6
- queries: bfloat16 [8192, 4096], P(('parts', 'ctx')), parts along dimension 0, may hold values from -360 to 360
- w_key: bfloat16 [8192, 512], P('ctx'), may hold values from -0.0625 to 0.0625
- w_value: bfloat16 [8192, 512], P('ctx'), may hold values from -0.0625 to 0.0625
- doc_ids: int32 [8192], P(('parts', 'ctx')), parts along dimension 0, may hold values from 0 to 7, never falling along the last dimension, each value on 1 to 1024 neighbouring positions
Outputs:
- attended: bfloat16 [8192, 4096], P(('parts', 'ctx')), parts along dimension 0
There are 2 independent parts, one for each index of `parts`. A program takes and returns all parts, laid end to end along the dimension named above; an argument that names none is the same for every part. Nothing has to cross between parts.
Inputs may be any that keep to these rules, and one draw needn't show every extreme that they name: doc_ids never fall along the sequence; each document has 1 to 1024 tokens and one has exactly 1024.
All inputs are finite; a program needn't handle non-finite values.
Results may differ from a plain program's by a relative error of at most 0.004.
The roundings to bfloat16 on the way count: a program that leaves them out, or rounds other values in their place, can miss the bound.
Values may be sent and summed in bfloat16 or wider, within the bound.
A program may use at most 128 MiB of HBM per device.

v0:
```python
import jax
import jax.numpy as jnp
from jax import lax
from jax.sharding import PartitionSpec as P

HEAD_DIM = 128
HEADS = 32
KV_HEADS = 4
REACH = 4


def from_behind(value, axis, steps):
    count = lax.axis_size(axis)
    leading, last = (max(0, -steps), min(count, count - steps))
    return lax.ppermute(value, axis, [(source, source + steps) for source in range(leading, last)])


def rotate(key_raw, positions):
    head_dim = HEAD_DIM
    half_dim = head_dim // 2
    inverse_freq = 500000.0 ** (-jnp.arange(half_dim).astype(jnp.float32) * 2.0 / head_dim)
    angles = positions.astype(jnp.float32)[:, None] * inverse_freq[None, :]
    cosine = jnp.cos(angles)[:, None, :]
    sine = jnp.sin(angles)[:, None, :]
    shaped = key_raw.reshape(key_raw.shape[0], KV_HEADS, head_dim)
    first_half = shaped[..., :half_dim]
    second_half = shaped[..., half_dim:]
    turned = jnp.concatenate(
        [first_half * cosine - second_half * sine, second_half * cosine + first_half * sine], -1
    )
    return turned.reshape(key_raw.shape[0], KV_HEADS * head_dim)


def attend(query_rows, key_rows, value_rows, allowed):
    group_size = HEADS // KV_HEADS
    num_q = query_rows.shape[0]
    num_k = key_rows.shape[0]
    q_heads = query_rows.reshape(num_q, KV_HEADS, group_size, HEAD_DIM).transpose(1, 0, 2, 3)
    k_heads = key_rows.reshape(num_k, KV_HEADS, HEAD_DIM).transpose(1, 0, 2)
    v_heads = value_rows.reshape(num_k, KV_HEADS, HEAD_DIM).transpose(1, 0, 2)

    def one_head(packed):
        q_one, k_one, v_one = packed
        scores = jnp.einsum(
            "bgd,kd->gbk", q_one, k_one, preferred_element_type=jnp.float32
        ) / jnp.sqrt(jnp.float32(HEAD_DIM))
        scores = jnp.where(allowed[None], scores, -jnp.inf)
        row_max = jnp.max(scores, -1, keepdims=True)
        expo = jnp.exp(scores - row_max)
        probs = (expo / jnp.sum(expo, -1, keepdims=True)).astype(jnp.bfloat16)
        return jnp.einsum("gbk,kd->bgd", probs, v_one, preferred_element_type=jnp.float32)

    result = lax.map(one_head, (q_heads, k_heads, v_heads))
    return result.transpose(1, 0, 2, 3).reshape(num_q, HEADS * HEAD_DIM).astype(jnp.bfloat16)


def on_device(hidden_states, queries, w_key, w_value, doc_ids):
    tok_rows = hidden_states.shape[0]
    hidden_f32 = hidden_states.astype(jnp.float32)
    normed = (
        hidden_f32 * lax.rsqrt(jnp.mean(hidden_f32 * hidden_f32, -1, keepdims=True) + 1e-05)
    ).astype(jnp.bfloat16)
    full_key, full_value = (
        lax.all_gather(w_key, "ctx", axis=0, tiled=True),
        lax.all_gather(w_value, "ctx", axis=0, tiled=True),
    )
    key_raw = jnp.dot(normed, full_key, preferred_element_type=jnp.float32)
    value_raw = jnp.dot(normed, full_value, preferred_element_type=jnp.float32)
    first_pos = lax.axis_index("ctx") * tok_rows
    positions = first_pos + jnp.arange(tok_rows)
    key_block = rotate(key_raw, positions).astype(jnp.bfloat16)
    value_block = value_raw.astype(jnp.bfloat16)
    key_list = [key_block]
    value_list = [value_block]
    doc_list = [doc_ids]
    pos_list = [positions]
    for offset in range(1, REACH + 1):
        arrived = from_behind((key_block, value_block, doc_ids), "ctx", offset)
        key_list.append(arrived[0])
        value_list.append(arrived[1])
        doc_list.append(arrived[2])
        pos_list.append(positions - offset * tok_rows)
    key_rows = jnp.concatenate(key_list, 0)
    value_rows = jnp.concatenate(value_list, 0)
    key_docs = jnp.concatenate(doc_list, 0)
    key_pos = jnp.concatenate(pos_list, 0)
    allowed = (
        (key_docs[None, :] == doc_ids[:, None])
        & (key_pos[None, :] <= positions[:, None])
        & (key_pos[None, :] >= 0)
    )
    return attend(queries, key_rows, value_rows, allowed)


def solution(mesh):
    in_specs = (
        P(("parts", "ctx"), None),
        P(("parts", "ctx"), None),
        P("ctx", None),
        P("ctx", None),
        P(("parts", "ctx")),
    )
    out_specs = P(("parts", "ctx"), None)
    return jax.shard_map(
        on_device, mesh=mesh, in_specs=in_specs, out_specs=out_specs, check_vma=False
    )
```

profile of v0, /device:TPU:20, one launch (start us, length us, event | category | flops | bytes accessed | tf_op | source)
XLA Modules:
  0.0 272.8 jit_solution(17600638021143734273)
XLA Ops:
  6.5 0.0 all-gather.5.cloned.1.call-start
  6.5 0.7 all-gather.5.cloned.1.call-update
  7.3 0.0 all-gather.3.cloned.1.call-start
  7.3 0.7 all-gather.3.cloned.1.call-update
  8.0 1.9 collective-permute-start.4
  9.9 3.4 %collective-permute-start.5 = (s32[256]{0:T(256)}, s32[256]{0:T(256)S(1)}, u32[]{:S(2)}, u32[]{:S(2)}) collective-permute-start(s32[256]{0:T(256)} %param.11), channel_id=1, source_target_pairs={{0,2},{1,3},{2,4},{3,5},{4,6},{5,7},{6,8},{7,9},{8,10},{9,11},{10,... | collective-permute-start | bytes 3080 | tf_op jit(solution)/shard_map/ppermute | solution.py:15
  13.4 3.1 %collective-permute-start.6 = (s32[256]{0:T(256)}, s32[256]{0:T(256)S(1)}, u32[]{:S(2)}, u32[]{:S(2)}) collective-permute-start(s32[256]{0:T(256)} %param.11), channel_id=1, source_target_pairs={{0,3},{1,4},{2,5},{3,6},{4,7},{5,8},{6,9},{7,10},{8,11},{9,12},{10... | collective-permute-start | bytes 3080 | tf_op jit(solution)/shard_map/ppermute | solution.py:15
  16.5 1.9 collective-permute-start.7
  18.6 0.0 copy-start.3
  18.6 0.0 copy-start
  18.6 3.5 %fusion.51 = f32[256]{0:T(256)S(1)} fusion(bf16[256,8192]{1,0:T(8,128)(2,1)} %param.7), kind=kLoop, calls=%fused_computation.36 | loop fusion | flops 6291200 | bytes 4195328 | tf_op jit(solution)/shard_map/reduce_sum | solution.py:61
  22.1 0.5 multiply_cosine_fusion
  22.6 0.0 copy-done.3
  22.6 0.0 copy-done
  22.7 2.5 copy.12
  25.1 0.0 collective-permute-done.4
  25.1 0.0 collective-permute-done.5
  25.1 0.0 collective-permute-done.6
  25.2 58.6 %all-gather.5.cloned.1.call-done = bf16[8192,512]{1,0:T(8,128)(2,1)} async-done(((bf16[512,512]{1,0:T(8,128)(2,1)}), bf16[8192,512]{1,0:T(8,128)(2,1)}) %all-gather.5.cloned.1.call-update) | async-done | bytes 8388624 | tf_op jit(solution)/shard_map/all_gather | solution.py:64
  83.7 7.0 %fusion.53 = f32[256,512]{1,0:T(8,128)S(1)} fusion(bf16[8192,512]{1,0:T(8,128)(2,1)} %all-gather.5.cloned.1.call-done, bf16[256,8192]{1,0:T(8,128)(2,1)} %param.7, f32[256]{0:T(256)S(1)} %add_rsqrt_fusion), kind=kOutput, calls=%fused_computation.38 | convolution fusion | flops 2153775104 | bytes 13108224 | tf_op jit(solution)/shard_map/dot_general | solution.py:67
  90.7 0.2 reshape.124
  90.9 0.5 subtract_convert_fusion
  91.5 0.4 pad_maximum_fusion
  91.8 0.9 copy.11
  92.7 2.2 collective-permute-start.8
  94.9 67.0 %all-gather.3.cloned.1.call-done = bf16[8192,512]{1,0:T(8,128)(2,1)} async-done(((bf16[512,512]{1,0:T(8,128)(2,1)}), bf16[8192,512]{1,0:T(8,128)(2,1)}) %all-gather.3.cloned.1.call-update) | async-done | bytes 8388624 | tf_op jit(solution)/shard_map/all_gather | solution.py:65
  161.9 7.0 %constant_dynamic-update-slice_fusion.4 = (bf16[1280,512]{1,0:T(8,128)(2,1)S(1)}, bf16[256,512]{1,0:T(8,128)(2,1)S(1)}) fusion(bf16[8192,512]{1,0:T(8,128)(2,1)} %all-gather.3.cloned.1.call-done, bf16[256,8192]{1,0:T(8,128)(2,1)} %param.7, f32[256]{0:T(256)S(1)} %add_rsqrt_fusion), kind=kOutput, calls=%fused_computation.50 | convolution fusion | flops 2153906176 | bytes 13108224 | tf_op jit(solution)/shard_map/dot_general | solution.py:68
  168.9 2.2 collective-permute-start
  171.1 0.0 collective-permute-done.7
  171.1 3.4 %collective-permute-start.1 = (bf16[256,512]{1,0:T(8,128)(2,1)S(1)}, bf16[256,512]{1,0:T(8,128)(2,1)S(1)}, u32[]{:S(2)}, u32[]{:S(2)}) collective-permute-start(bf16[256,512]{1,0:T(8,128)(2,1)S(1)} %get-tuple-element.100), channel_id=1, source_target_pairs={{0,2},{1,3},{2,4},{3,5},{4,6},{5,7},{6,8},{7,9},{8,10},{9,11},{10,... | collective-permute-start | bytes 786440 | tf_op jit(solution)/shard_map/ppermute | solution.py:15
  174.4 1.0 constant_dynamic-update-slice_fusion.9
  175.4 2.6 collective-permute-start.9
  178.0 1.9 collective-permute-start.10
  179.9 0.0 collective-permute-done.8
  179.9 1.9 collective-permute-start.2
  181.9 0.0 collective-permute-done
  181.9 1.9 collective-permute-start.3
  183.9 0.0 collective-permute-done.1
  183.9 2.1 collective-permute-start.11
  186.0 13.9 %collective-permute-done.2 = bf16[256,512]{1,0:T(8,128)(2,1)S(1)} collective-permute-done((bf16[256,512]{1,0:T(8,128)(2,1)S(1)}, bf16[256,512]{1,0:T(8,128)(2,1)S(1)}, u32[]{:S(2)}, u32[]{:S(2)}) %collective-permute-start.2) | collective-permute-done | bytes 262176 | tf_op jit(solution)/shard_map/ppermute | solution.py:15
  199.9 5.7 %collective-permute-done.3 = bf16[256,512]{1,0:T(8,128)(2,1)S(1)} collective-permute-done((bf16[256,512]{1,0:T(8,128)(2,1)S(1)}, bf16[256,512]{1,0:T(8,128)(2,1)S(1)}, u32[]{:S(2)}, u32[]{:S(2)}) %collective-permute-start.3) | collective-permute-done | bytes 262176 | tf_op jit(solution)/shard_map/ppermute | solution.py:15
  205.6 0.0 copy-done.2
  205.6 0.0 copy-start.1
  205.6 1.5 copy.17
  207.1 0.0 collective-permute-done.9
  207.1 1.7 constant_dynamic-update-slice_fusion.7
  208.8 0.0 collective-permute-done.10
  208.8 1.7 constant_dynamic-update-slice_fusion.6
  210.5 0.8 collective-permute-done.11
  211.3 1.7 constant_dynamic-update-slice_fusion.5
  213.0 48.9 %while.11 = (s32[]{:T(128)}, bf16[4,256,8,128]{1,3,2,0:T(8,128)(2,1)}, bf16[4,1280,128]{1,2,0:T(8,128)(2,1)}, bf16[4,1280,128]{1,2,0:T(8,128)(2,1)}, bf16[4,256,...) while((s32[]{:T(128)}, ...), condition=%wide.region_4.5_spmd.clone, body=%wide.region_1.4_spmd.clone.sunk | while | flops 2038174208 | bytes 4096365 | solution.py:53
  213.0 1.1 and_and_fusion.2
  214.0 4.4 %fusion.80 = f32[8,256]{1,0:T(8,128)S(1)} fusion(pred[256,1280]{0,1:T(8,128)(4,1)S(1)} %and_and_fusion.2, bf16[4,256,8,128]{1,3,2,0:T(8,128)(2,1)S(1)} %get-tuple-element.190, s32[]{:T(128)} %get-tuple-element.175, bf16[4,1280,128]{1,2,0:T(8,128)(2,1)} %get-tuple-element.189), kind=kOutput, calls=%fused_computation.71.clone.1 | convolution fusion | flops 681575680 | bytes 1188864 | tf_op jit(solution)/shard_map/while/body/eval_jaxpr/sub | solution.py:49
  218.5 6.7 %fusion.81 = bf16[4,256,8,128]{1,3,2,0:T(8,128)(2,1)} fusion(bf16[4,256,8,128]{1,3,2,0:T(8,128)(2,1)} %get-tuple-element.176, s32[]{:T(128)} %get-tuple-element.175, f32[8,256]{1,0:T(8,128)S(1)} %fusion.80, pred[256,1280]{0,1:T(8,128)(4,1)S(1)} %and_and_fusion.2, bf16[4,256,8,128]{1,3,2,0:T(8,128)(2,1)S(1)} %get-tuple-element.190, ...), kind=kOutput, calls=%fused_computation.12.clone.1 | convolution fusion | flops 1355287808 | bytes 2566144 | tf_op jit(solution)/shard_map/while/body/eval_jaxpr/gbk,kd->bgd/dot_general | solution.py:51
  225.2 1.1 and_and_fusion.2
  226.2 4.4 %fusion.80 = f32[8,256]{1,0:T(8,128)S(1)} fusion(pred[256,1280]{0,1:T(8,128)(4,1)S(1)} %and_and_fusion.2, bf16[4,256,8,128]{1,3,2,0:T(8,128)(2,1)S(1)} %get-tuple-element.190, s32[]{:T(128)} %get-tuple-element.175, bf16[4,1280,128]{1,2,0:T(8,128)(2,1)} %get-tuple-element.189), kind=kOutput, calls=%fused_computation.71.clone.1 | convolution fusion | flops 681575680 | bytes 1188864 | tf_op jit(solution)/shard_map/while/body/eval_jaxpr/sub | solution.py:49
  230.7 6.7 %fusion.81 = bf16[4,256,8,128]{1,3,2,0:T(8,128)(2,1)} fusion(bf16[4,256,8,128]{1,3,2,0:T(8,128)(2,1)} %get-tuple-element.176, s32[]{:T(128)} %get-tuple-element.175, f32[8,256]{1,0:T(8,128)S(1)} %fusion.80, pred[256,1280]{0,1:T(8,128)(4,1)S(1)} %and_and_fusion.2, bf16[4,256,8,128]{1,3,2,0:T(8,128)(2,1)S(1)} %get-tuple-element.190, ...), kind=kOutput, calls=%fused_computation.12.clone.1 | convolution fusion | flops 1355287808 | bytes 2566144 | tf_op jit(solution)/shard_map/while/body/eval_jaxpr/gbk,kd->bgd/dot_general | solution.py:51
  237.4 1.1 and_and_fusion.2
  238.4 4.4 %fusion.80 = f32[8,256]{1,0:T(8,128)S(1)} fusion(pred[256,1280]{0,1:T(8,128)(4,1)S(1)} %and_and_fusion.2, bf16[4,256,8,128]{1,3,2,0:T(8,128)(2,1)S(1)} %get-tuple-element.190, s32[]{:T(128)} %get-tuple-element.175, bf16[4,1280,128]{1,2,0:T(8,128)(2,1)} %get-tuple-element.189), kind=kOutput, calls=%fused_computation.71.clone.1 | convolution fusion | flops 681575680 | bytes 1188864 | tf_op jit(solution)/shard_map/while/body/eval_jaxpr/sub | solution.py:49
  242.9 6.8 %fusion.81 = bf16[4,256,8,128]{1,3,2,0:T(8,128)(2,1)} fusion(bf16[4,256,8,128]{1,3,2,0:T(8,128)(2,1)} %get-tuple-element.176, s32[]{:T(128)} %get-tuple-element.175, f32[8,256]{1,0:T(8,128)S(1)} %fusion.80, pred[256,1280]{0,1:T(8,128)(4,1)S(1)} %and_and_fusion.2, bf16[4,256,8,128]{1,3,2,0:T(8,128)(2,1)S(1)} %get-tuple-element.190, ...), kind=kOutput, calls=%fused_computation.12.clone.1 | convolution fusion | flops 1355287808 | bytes 2566144 | tf_op jit(solution)/shard_map/while/body/eval_jaxpr/gbk,kd->bgd/dot_general | solution.py:51
  249.6 1.1 and_and_fusion.2
  250.7 4.4 %fusion.80 = f32[8,256]{1,0:T(8,128)S(1)} fusion(pred[256,1280]{0,1:T(8,128)(4,1)S(1)} %and_and_fusion.2, bf16[4,256,8,128]{1,3,2,0:T(8,128)(2,1)S(1)} %get-tuple-element.190, s32[]{:T(128)} %get-tuple-element.175, bf16[4,1280,128]{1,2,0:T(8,128)(2,1)} %get-tuple-element.189), kind=kOutput, calls=%fused_computation.71.clone.1 | convolution fusion | flops 681575680 | bytes 1188864 | tf_op jit(solution)/shard_map/while/body/eval_jaxpr/sub | solution.py:49
  255.1 6.7 %fusion.81 = bf16[4,256,8,128]{1,3,2,0:T(8,128)(2,1)} fusion(bf16[4,256,8,128]{1,3,2,0:T(8,128)(2,1)} %get-tuple-element.176, s32[]{:T(128)} %get-tuple-element.175, f32[8,256]{1,0:T(8,128)S(1)} %fusion.80, pred[256,1280]{0,1:T(8,128)(4,1)S(1)} %and_and_fusion.2, bf16[4,256,8,128]{1,3,2,0:T(8,128)(2,1)S(1)} %get-tuple-element.190, ...), kind=kOutput, calls=%fused_computation.12.clone.1 | convolution fusion | flops 1355287808 | bytes 2566144 | tf_op jit(solution)/shard_map/while/body/eval_jaxpr/gbk,kd->bgd/dot_general | solution.py:51
  261.8 4.1 %copy.18 = bf16[256,4096]{1,0:T(8,128)(2,1)} copy(bf16[256,4096]{0,1:T(8,128)(2,1)} %bitcast.82) | data formatting | bytes 4194304 | tf_op jit(solution)/shard_map/convert_element_type | solution.py:54
  (24 shorter events, 0.2 us)
Async XLA Ops:
  6.5 77.2 %all-gather.5.cloned.1.call-start = ((), (), s32[]{:S(2)}) async-start(), calls=%async_computation.1 | async-start | bytes 8912896 | tf_op jit(solution)/shard_map/all_gather | solution.py:64
  7.3 154.6 %all-gather.3.cloned.1.call-start = ((), (), s32[]{:S(2)}) async-start(), calls=%async_computation | async-start | bytes 8912896 | tf_op jit(solution)/shard_map/all_gather | solution.py:65
  8.0 17.1 %collective-permute-start.4 = (s32[256]{0:T(256)}, s32[256]{0:T(256)S(1)}, u32[]{:S(2)}, u32[]{:S(2)}) collective-permute-start(s32[256]{0:T(256)} %param.11), channel_id=1, source_target_pairs={{0,1},{1,2},{2,3},{3,4},{4,5},{5,6},{6,7},{7,8},{8,9},{9,10},{10,1... | collective-permute-start | bytes 3080 | tf_op jit(solution)/shard_map/ppermute | solution.py:15
  9.9 15.2 %collective-permute-start.5 = (s32[256]{0:T(256)}, s32[256]{0:T(256)S(1)}, u32[]{:S(2)}, u32[]{:S(2)}) collective-permute-start(s32[256]{0:T(256)} %param.11), channel_id=1, source_target_pairs={{0,2},{1,3},{2,4},{3,5},{4,6},{5,7},{6,8},{7,9},{8,10},{9,11},{10,... | collective-permute-start | bytes 3080 | tf_op jit(solution)/shard_map/ppermute | solution.py:15
  13.4 11.8 %collective-permute-start.6 = (s32[256]{0:T(256)}, s32[256]{0:T(256)S(1)}, u32[]{:S(2)}, u32[]{:S(2)}) collective-permute-start(s32[256]{0:T(256)} %param.11), channel_id=1, source_target_pairs={{0,3},{1,4},{2,5},{3,6},{4,7},{5,8},{6,9},{7,10},{8,11},{9,12},{10... | collective-permute-start | bytes 3080 | tf_op jit(solution)/shard_map/ppermute | solution.py:15
  16.5 154.5 %collective-permute-start.7 = (s32[256]{0:T(256)}, s32[256]{0:T(256)S(1)}, u32[]{:S(2)}, u32[]{:S(2)}) collective-permute-start(s32[256]{0:T(256)} %param.11), channel_id=1, source_target_pairs={{0,4},{1,5},{2,6},{3,7},{4,8},{5,9},{6,10},{7,11},{8,12},{9,13},{1... | collective-permute-start | bytes 3080 | tf_op jit(solution)/shard_map/ppermute | solution.py:15
  18.6 4.0 %copy-start.3 = (s32[256]{0:T(256)S(1)}, s32[256]{0:T(256)}, u32[]{:S(2)}) copy-start(s32[256]{0:T(256)} %param.11) | copy-start | bytes 3076
  18.6 4.1 %copy-start = (bf16[256,4096]{1,0:T(8,128)(2,1)S(1)}, bf16[256,4096]{1,0:T(8,128)(2,1)}, u32[]{:S(2)}) copy-start(bf16[256,4096]{1,0:T(8,128)(2,1)} %param.8) | copy-start | bytes 6291460
  92.7 87.2 %collective-permute-start.8 = (bf16[256,512]{0,1:T(8,128)(2,1)}, bf16[256,512]{0,1:T(8,128)(2,1)S(1)}, u32[]{:S(2)}, u32[]{:S(2)}) collective-permute-start(bf16[256,512]{0,1:T(8,128)(2,1)} %bitcast.2), channel_id=1, source_target_pairs={{0,1},{1,2},{2,3},{3,4},{4,5},{5,6},{6,7},{7,8},{8,9},{9,10},{10,1... | collective-permute-start | bytes 786440 | tf_op jit(solution)/shard_map/ppermute | solution.py:15
  168.9 13.0 %collective-permute-start = (bf16[256,512]{1,0:T(8,128)(2,1)S(1)}, bf16[256,512]{1,0:T(8,128)(2,1)S(1)}, u32[]{:S(2)}, u32[]{:S(2)}) collective-permute-start(bf16[256,512]{1,0:T(8,128)(2,1)S(1)} %get-tuple-element.100), channel_id=1, source_target_pairs={{0,1},{1,2},{2,3},{3,4},{4,5},{5,6},{6,7},{7,8},{8,9},{9,10},{10,1... | collective-permute-start | bytes 786440 | tf_op jit(solution)/shard_map/ppermute | solution.py:15
  171.1 12.8 %collective-permute-start.1 = (bf16[256,512]{1,0:T(8,128)(2,1)S(1)}, bf16[256,512]{1,0:T(8,128)(2,1)S(1)}, u32[]{:S(2)}, u32[]{:S(2)}) collective-permute-start(bf16[256,512]{1,0:T(8,128)(2,1)S(1)} %get-tuple-element.100), channel_id=1, source_target_pairs={{0,2},{1,3},{2,4},{3,5},{4,6},{5,7},{6,8},{7,9},{8,10},{9,11},{10,... | collective-permute-start | bytes 786440 | tf_op jit(solution)/shard_map/ppermute | solution.py:15
  175.4 31.7 %collective-permute-start.9 = (bf16[256,512]{0,1:T(8,128)(2,1)}, bf16[256,512]{0,1:T(8,128)(2,1)}, u32[]{:S(2)}, u32[]{:S(2)}) collective-permute-start(bf16[256,512]{0,1:T(8,128)(2,1)} %bitcast.2), channel_id=1, source_target_pairs={{0,2},{1,3},{2,4},{3,5},{4,6},{5,7},{6,8},{7,9},{8,10},{9,11},{10,... | collective-permute-start | bytes 786440 | tf_op jit(solution)/shard_map/ppermute | solution.py:15
  178.0 30.8 %collective-permute-start.10 = (bf16[256,512]{0,1:T(8,128)(2,1)}, bf16[256,512]{0,1:T(8,128)(2,1)}, u32[]{:S(2)}, u32[]{:S(2)}) collective-permute-start(bf16[256,512]{0,1:T(8,128)(2,1)} %bitcast.2), channel_id=1, source_target_pairs={{0,3},{1,4},{2,5},{3,6},{4,7},{5,8},{6,9},{7,10},{8,11},{9,12},{10... | collective-permute-start | bytes 786440 | tf_op jit(solution)/shard_map/ppermute | solution.py:15
  179.9 20.0 %collective-permute-start.2 = (bf16[256,512]{1,0:T(8,128)(2,1)S(1)}, bf16[256,512]{1,0:T(8,128)(2,1)S(1)}, u32[]{:S(2)}, u32[]{:S(2)}) collective-permute-start(bf16[256,512]{1,0:T(8,128)(2,1)S(1)} %get-tuple-element.100), channel_id=1, source_target_pairs={{0,3},{1,4},{2,5},{3,6},{4,7},{5,8},{6,9},{7,10},{8,11},{9,12},{10... | collective-permute-start | bytes 786440 | tf_op jit(solution)/shard_map/ppermute | solution.py:15
  181.9 23.7 %copy-start.2 = (bf16[1280,512]{0,1:T(8,128)(2,1)}, bf16[1280,512]{0,1:T(8,128)(2,1)S(1)}, u32[]{:S(2)}) copy-start(bf16[1280,512]{0,1:T(8,128)(2,1)S(1)} %constant_dynamic-update-slice_fusion.8) | copy-start | bytes 3932164
  181.9 23.7 %collective-permute-start.3 = (bf16[256,512]{1,0:T(8,128)(2,1)S(1)}, bf16[256,512]{1,0:T(8,128)(2,1)S(1)}, u32[]{:S(2)}, u32[]{:S(2)}) collective-permute-start(bf16[256,512]{1,0:T(8,128)(2,1)S(1)} %get-tuple-element.100), channel_id=1, source_target_pairs={{0,4},{1,5},{2,6},{3,7},{4,8},{5,9},{6,10},{7,11},{8,12},{9,13},{1... | collective-permute-start | bytes 786440 | tf_op jit(solution)/shard_map/ppermute | solution.py:15
  183.9 27.4 %collective-permute-start.11 = (bf16[256,512]{0,1:T(8,128)(2,1)}, bf16[256,512]{0,1:T(8,128)(2,1)}, u32[]{:S(2)}, u32[]{:S(2)}) collective-permute-start(bf16[256,512]{0,1:T(8,128)(2,1)} %bitcast.2), channel_id=1, source_target_pairs={{0,4},{1,5},{2,6},{3,7},{4,8},{5,9},{6,10},{7,11},{8,12},{9,13},{1... | collective-permute-start | bytes 786440 | tf_op jit(solution)/shard_map/ppermute | solution.py:15
  205.6 7.4 %copy-start.1 = (bf16[256,4096]{0,1:T(8,128)(2,1)S(1)}, bf16[256,4096]{0,1:T(8,128)(2,1)}, u32[]{:S(2)}) copy-start(bf16[256,4096]{0,1:T(8,128)(2,1)} %copy.12) | copy-start | bytes 6291460
Sparse Core Ops, SparseCore 0:
  9.5 74.1 all-gather.4
  85.9 75.9 all-gather.2
where the time goes:
time: 274 us; the launch traced here: 273 us
  waiting for transfers between devices  147 us (54%)
  matrix products  58.6 us (21%)
  starting transfers between devices  28.6 us (10%)
  local copies, waits for them, and re-layouts  15.2 us (6%)
  between operations  13.8 us (5%)
  other arithmetic  9.15 us (3%)
    all_gather x1, waiting for transfers between devices, on_device(): lax.all_gather(w_value, 'ctx', axis=0, tiled=True)  67 us
    all_gather x1, waiting for transfers between devices, on_device(): lax.all_gather(w_key, 'ctx', axis=0, tiled=True)  58.6 us
    ppermute x12, starting transfers between devices, from_behind(): lax.ppermute(value, axis, [(source, source + steps) for source in range(l...  28.5 us
    dot_general x4, matrix products, one_head(): jnp.einsum('gbk,kd->bgd', probs, v_one, preferred_element_type=jnp.float32)  26.9 us
    ppermute x12, waiting for transfers between devices, from_behind(): lax.ppermute(value, axis, [(source, source + steps) for source in range(l...  20.4 us
    sub x4, matrix products, one_head(): expo = jnp.exp(scores - row_max)  17.7 us
    dot_general x1, matrix products, on_device(): value_raw = jnp.dot(normed, full_value, preferred_element_type=jnp.float32)  7.02 us
    dot_general x1, matrix products, on_device(): key_raw = jnp.dot(normed, full_key, preferred_element_type=jnp.float32)  7.01 us
  transfers between devices with their start and end apart: 14, of which 5 were waited for; matrix products, arithmetic and copies ran while one was open for 10% of the time, Pallas kernels for 0%

commit v1 on v0

v1 whole, which is shorter than its diff:
```python
import functools
import math

import jax
import jax.numpy as jnp
from jax import lax
from jax.experimental import pallas as pl
from jax.experimental.pallas import tpu as pltpu
from jax.sharding import PartitionSpec as P

HEAD_DIM = 128
HEADS = 32
KV_HEADS = 4
REACH = 4
GROUP = HEADS // KV_HEADS
MESH = pl.DeviceIdType.MESH


def project_kernel(n, parts, hidden, wk, wv, cos2, sin2, doc, kout, vout, dout,
                   w_all, normed, acc, own_sem, ring_s, ring_r, sib_s, sib_r, x_s, x_r,
                   xs_s, xs_r, ex_s, ex_r, doc_s, doc_r):
    chips = n // 2
    rows = wk.shape[0]
    half = rows // 2
    third = (half // 48) * 16 if parts == 2 else 0
    length = half - third
    tok = hidden.shape[0]
    depth = hidden.shape[1]

    idx = lax.axis_index("ctx")
    part = lax.axis_index("parts")
    core = idx % 2
    chip_no = idx // 2
    col = chip_no % 2
    lane = chip_no // 2
    pos = col * (chips - 1 - lane) + (1 - col) * lane
    sibling = idx + 1 - 2 * core

    def chip_at(place):
        upper = place // (chips // 2)
        return (1 - upper) * 2 * place + upper * (2 * (chips - 1 - place) + 1)

    def base(d, s, which_core):
        owner = (pos + chips - s) % chips if d == 0 else (pos + s) % chips
        return (2 * chip_at(owner) + which_core) * rows + d * half

    def at(m, start, count):
        return w_all.at[m, pl.ds(pl.multiple_of(start, 16), count), :]

    def ring(m, d, s, recv_s):
        target = (pos + 1) % chips if d == 0 else (pos + chips - 1) % chips
        piece = at(m, base(d, s, core) + part * third, length)
        return pltpu.make_async_remote_copy(
            piece, piece, ring_s.at[m, d, s], ring_r.at[m, d, recv_s],
            device_id={"ctx": 2 * chip_at(target) + core}, device_id_type=MESH)

    def sib_own(m, d, which_core):
        piece = at(m, base(d, 0, which_core), half)
        return pltpu.make_async_remote_copy(
            piece, piece, sib_s.at[m, d, 0], sib_r.at[m, d, 0],
            device_id={"ctx": sibling}, device_id_type=MESH)

    def sib(m, d, s, which_core):
        piece = at(m, base(d, s, which_core) + part * third, length)
        return pltpu.make_async_remote_copy(
            piece, piece, sib_s.at[m, d, s], sib_r.at[m, d, s],
            device_id={"ctx": sibling}, device_id_type=MESH)

    def cross(m, d, s, of_part):
        piece = at(m, base(d, s, core) + of_part * (half - third), third)
        return pltpu.make_async_remote_copy(
            piece, piece, x_s.at[m, d, s], x_r.at[m, d, s],
            device_id={"parts": 1 - part}, device_id_type=MESH)

    def cross_sib(m, d, s, which_core):
        piece = at(m, base(d, s, which_core) + (1 - part) * (half - third), third)
        return pltpu.make_async_remote_copy(
            piece, piece, xs_s.at[m, d, s], xs_r.at[m, d, s],
            device_id={"ctx": sibling}, device_id_type=MESH)

    def send_docs(o):
        return pltpu.make_async_remote_copy(
            doc, dout.at[o], doc_s.at[o - 1], doc_r.at[o - 1],
            device_id={"ctx": (idx + o) % n}, device_id_type=MESH)

    def send_ahead(m, buf, o):
        return pltpu.make_async_remote_copy(
            buf.at[0], buf.at[o], ex_s.at[m, o - 1], ex_r.at[m, o - 1],
            device_id={"ctx": (idx + o) % n}, device_id_type=MESH)

    def send_beside(m, buf, o):
        return pltpu.make_async_remote_copy(
            buf.at[o - 1 + 2 * core], buf.at[o], ex_s.at[m, o - 1],
            ex_r.at[m, o - 1], device_id={"ctx": sibling}, device_id_type=MESH)

    own = []
    for m, w in ((0, wk), (1, wv)):
        copy = pltpu.make_async_copy(w, at(m, idx * rows, rows), own_sem.at[m])
        copy.start()
        own.append(copy)

    barrier = pltpu.get_barrier_semaphore()
    greeted = [{"ctx": (idx + o) % n} for o in range(1, REACH + 1)]
    greeted += [{"ctx": (idx + n - o) % n} for o in range(1, REACH + 1)]
    greeted += [{"ctx": 2 * chip_at((pos + o) % chips) + core} for o in (1, chips - 1)]
    greeted += [{"ctx": sibling}]
    if third:
        greeted += [{"parts": 1 - part}]
    for who in greeted:
        pl.semaphore_signal(barrier, inc=1, device_id=who, device_id_type=MESH)
    pl.semaphore_wait(barrier, len(greeted))

    streams = [(m, d) for m in (0, 1) for d in (0, 1)]
    own[0].wait()
    own[1].wait()
    for m, d in streams:
        ring(m, d, 0, 1).start()
    for m, d in streams:
        sib_own(m, d, core).start()
    for o in range(1, REACH + 1):
        @pl.when(idx + o < n)
        def _():
            send_docs(o).start()

        @pl.when(idx < o)
        def _():
            kout[o] = jnp.zeros(kout.shape[1:], kout.dtype)
            vout[o] = jnp.zeros(vout.shape[1:], vout.dtype)
            dout[o] = jnp.full(dout.shape[1:], -1, dout.dtype)
    dout[0] = doc[...]

    @pl.loop(0, tok // 16)
    def _(i):
        r16 = pl.ds(pl.multiple_of(i * 16, 16), 16)
        x = hidden[r16, :].astype(jnp.float32)
        mean = jnp.sum(x * x, -1, keepdims=True) * (1.0 / depth)
        normed[r16, :] = (x * lax.rsqrt(mean + 1e-05)).astype(jnp.bfloat16)

    @pl.loop(1, chips)
    def _(s):
        for m, d in streams:
            ring(m, d, s, s).wait_recv()

            @pl.when(s < chips - 1)
            def _():
                ring(m, d, s, s + 1).start()

            if third:
                cross(m, d, s, part).start()
            sib(m, d, s, core).start()
        if third:
            @pl.when(s > 1)
            def _():
                for m, d in streams:
                    cross(m, d, s - 1, 1 - part).wait_recv()
                    cross_sib(m, d, s - 1, core).start()

    if third:
        for m, d in streams:
            cross(m, d, chips - 1, 1 - part).wait_recv()
            cross_sib(m, d, chips - 1, core).start()

    for m, d in streams:
        sib_own(m, d, 1 - core).wait_recv()

    @pl.loop(1, chips)
    def _(s):
        for m, d in streams:
            sib(m, d, s, 1 - core).wait_recv()
            if third:
                cross_sib(m, d, s, 1 - core).wait_recv()

    step = 1024
    for m in (0, 1):
        for i in range(depth // step):
            part_sum = jnp.dot(normed[:, i * step:(i + 1) * step],
                               w_all[m, i * step:(i + 1) * step, :],
                               preferred_element_type=jnp.float32)
            acc[...] = part_sum if i == 0 else acc[...] + part_sum
        if m == 0:
            for h in range(KV_HEADS):
                cols = slice(h * HEAD_DIM, (h + 1) * HEAD_DIM)
                x = acc[:, cols]
                turned = x * cos2[...] + pltpu.roll(x, HEAD_DIM // 2, 1) * sin2[...]
                kout[0, :, cols] = turned.astype(jnp.bfloat16)
        else:
            vout[0] = acc[...].astype(jnp.bfloat16)
        buf = (kout, vout)[m]
        for o in (2, 4):
            @pl.when(idx + o < n)
            def _():
                send_ahead(m, buf, o).start()

    for m, buf in ((0, kout), (1, vout)):
        for o in (2, 4):
            @pl.when(idx >= o)
            def _():
                send_ahead(m, buf, o).wait_recv()
        for o in (1, 3):
            @pl.when(sibling >= o)
            def _():
                send_beside(m, buf, o).start()
    for m, buf in ((0, kout), (1, vout)):
        for o in (1, 3):
            @pl.when(idx >= o)
            def _():
                send_beside(m, buf, o).wait_recv()

            @pl.when(sibling >= o)
            def _():
                send_beside(m, buf, o).wait_send()
        for o in (2, 4):
            @pl.when(idx + o < n)
            def _():
                send_ahead(m, buf, o).wait_send()
    for o in range(1, REACH + 1):
        @pl.when(idx + o < n)
        def _():
            send_docs(o).wait_send()

        @pl.when(idx >= o)
        def _():
            send_docs(o).wait_recv()

    for m, d in streams:
        ring(m, d, 0, 1).wait_send()
        sib_own(m, d, core).wait_send()

    @pl.loop(1, chips)
    def _(s):
        for m, d in streams:
            @pl.when(s < chips - 1)
            def _():
                ring(m, d, s, s).wait_send()

            sib(m, d, s, core).wait_send()
            if third:
                cross(m, d, s, part).wait_send()
                cross_sib(m, d, s, core).wait_send()


def attend_kernel(q, k, v, key_docs, q_docs, out, bias):
    tok = q.shape[0]
    span = k.shape[0]

    @pl.when(pl.program_id(0) == 0)
    def _():
        same = key_docs[...] == q_docs[...]
        key_at = lax.broadcasted_iota(jnp.int32, (tok, span), 1)
        row = lax.broadcasted_iota(jnp.int32, (tok, span), 0)
        allowed = same & (key_at <= row + jnp.where(key_at >= tok, span, 0))
        bias[...] = jnp.where(allowed, 0.0, -jnp.inf)

    scale = math.log2(math.e) / math.sqrt(HEAD_DIM)
    for g in range(GROUP):
        cols = slice(g * HEAD_DIM, (g + 1) * HEAD_DIM)
        scores = lax.dot_general(q[:, cols], k[...], (((1,), (1,)), ((), ())),
                                 preferred_element_type=jnp.float32) + bias[...]
        top = jnp.max(scores, -1, keepdims=True)
        expo = jnp.exp2((scores - top) * scale)
        total = jnp.sum(expo, -1, keepdims=True)
        probs = (expo * (1.0 / total)).astype(jnp.bfloat16)
        out[:, cols] = jnp.dot(
            probs, v[...], preferred_element_type=jnp.float32).astype(jnp.bfloat16)


def on_device(n, parts, hidden_states, queries, w_key, w_value, doc_ids):
    tok, depth = hidden_states.shape
    kvw = w_key.shape[1]
    half_dim = HEAD_DIM // 2
    inverse_freq = 500000.0 ** (-jnp.arange(half_dim).astype(jnp.float32) * 2.0 / HEAD_DIM)
    positions = lax.axis_index("ctx") * tok + jnp.arange(tok)
    angles = positions.astype(jnp.float32)[:, None] * inverse_freq[None, :]
    cosine, sine = jnp.cos(angles), jnp.sin(angles)
    cos2 = jnp.concatenate([cosine, cosine], -1)
    sin2 = jnp.concatenate([-sine, sine], -1)
    chips = n // 2
    sem = pltpu.SemaphoreType.DMA
    blocks = REACH + 1
    in_vmem = pl.BlockSpec(memory_space=pltpu.VMEM)
    in_any = pl.BlockSpec(memory_space=pl.ANY)
    keys, values, docs = pl.pallas_call(
        functools.partial(project_kernel, n, parts),
        out_shape=(
            jax.ShapeDtypeStruct((blocks, tok, kvw), jnp.bfloat16),
            jax.ShapeDtypeStruct((blocks, tok, kvw), jnp.bfloat16),
            jax.ShapeDtypeStruct((blocks, 1, tok), jnp.int32),
        ),
        in_specs=[in_vmem, in_any, in_any, in_vmem, in_vmem, in_vmem],
        out_specs=(in_vmem, in_vmem, in_vmem),
        scratch_shapes=[
            pltpu.VMEM((2, depth, kvw), jnp.bfloat16),
            pltpu.VMEM((tok, depth), jnp.bfloat16),
            pltpu.VMEM((tok, kvw), jnp.float32),
            sem((2,)),
        ] + [sem((2, 2, chips))] * 8 + [sem((2, REACH))] * 2 + [sem((REACH,))] * 2,
        compiler_params=pltpu.CompilerParams(
            collective_id=0, has_side_effects=True, vmem_limit_bytes=48 * 2**20),
        name="project",
    )(hidden_states, w_key, w_value, cos2, sin2, doc_ids.reshape(1, tok))
    span = blocks * tok
    width = GROUP * HEAD_DIM
    return pl.pallas_call(
        attend_kernel,
        grid=(KV_HEADS,),
        out_shape=jax.ShapeDtypeStruct(queries.shape, jnp.bfloat16),
        in_specs=[
            pl.BlockSpec((tok, width), lambda h: (0, h)),
            pl.BlockSpec((span, HEAD_DIM), lambda h: (0, h)),
            pl.BlockSpec((span, HEAD_DIM), lambda h: (0, h)),
            pl.BlockSpec((1, span), lambda h: (0, 0)),
            pl.BlockSpec((tok, 1), lambda h: (0, 0)),
        ],
        out_specs=pl.BlockSpec((tok, width), lambda h: (0, h)),
        scratch_shapes=[pltpu.VMEM((tok, span), jnp.float32)],
        compiler_params=pltpu.CompilerParams(vmem_limit_bytes=48 * 2**20),
        name="attend",
    )(queries, keys.reshape(span, kvw), values.reshape(span, kvw),
      docs.reshape(1, span), doc_ids.reshape(tok, 1))


def solution(mesh):
    in_specs = (
        P(("parts", "ctx"), None),
        P(("parts", "ctx"), None),
        P("ctx", None),
        P("ctx", None),
        P(("parts", "ctx")),
    )
    out_specs = P(("parts", "ctx"), None)
    return jax.shard_map(
        functools.partial(on_device, mesh.shape["ctx"], mesh.shape["parts"]),
        mesh=mesh, in_specs=in_specs, out_specs=out_specs, check_vma=False
    )
```

time: 274 us -> 129 us (0.47)
  waiting for transfers between devices: 147 us -> 0 us
  Pallas kernels: 0 us -> 123 us
  matrix products: 58.6 us -> 0 us
  starting transfers between devices: 28.6 us -> 0 us
  between operations: 13.8 us -> 0.05 us
  local copies, waits for them, and re-layouts: 15.2 us -> 3.57 us
  other arithmetic: 9.15 us -> 0.68 us
    all_gather x2 -> x0, waiting for transfers between devices: 126 us -> none  [the longest x1 67 us: on_device(): lax.all_gather(w_value, 'ctx', axis=0, tiled=True)]
    pallas_call x0 -> x2, Pallas kernels: none -> 123 us  [the longest x1 97 us: on_device(): pl.pallas_call(functools.partial(project_kernel, n, parts), out_shape=(ja...]
    dot_general x6 -> x0, matrix products: 40.9 us -> none  [the longest x4 26.9 us: one_head(): jnp.einsum('gbk,kd->bgd', probs, v_one, preferred_element_type=jnp.float32)]
    ppermute x12 -> x0, starting transfers between devices: 28.5 us -> none  [from_behind(): lax.ppermute(value, axis, [(source, source + steps) for source in range(l...]
    ppermute x12 -> x0, waiting for transfers between devices: 20.4 us -> none  [from_behind(): lax.ppermute(value, axis, [(source, source + steps) for source in range(l...]
    sub x4 -> x0, matrix products: 17.7 us -> none  [one_head(): expo = jnp.exp(scores - row_max)]
    and x4 -> x0, other arithmetic: 4.23 us -> none  [on_device(): (key_docs[None, :] == doc_ids[:, None]) & (key_pos[None, :] <= positions[...]
    unnamed x20 -> x8, local copies, waits for them, and re-layouts: 6.94 us -> 2.76 us
  transfers between devices with their start and end apart: 14 -> 0, of which waited for: 5 -> 0; matrix products, arithmetic and copies ran while one was open for 10% -> 0% of each run, Pallas kernels for 0% -> 0%
where the time goes in v1:
time: 129 us; the launch traced here: 128 us
  Pallas kernels  123 us (95%)
  local copies, waits for them, and re-layouts  3.57 us (3%)
    pallas_call x1, Pallas kernels, on_device(): pl.pallas_call(functools.partial(project_kernel, n, parts), out_shape=(ja...  97 us
    pallas_call x1, Pallas kernels, on_device(): pl.pallas_call(attend_kernel, grid=(KV_HEADS,), out_shape=jax.ShapeDtypeS...  26.3 us
    unnamed x8, local copies, waits for them, and re-layouts  2.76 us

profile of v1, /device:TPU:20, one launch (start us, length us, event | category | flops | bytes accessed | tf_op | source)
XLA Modules:
  0.0 127.6 jit_solution(3223701005185109828)
XLA Ops:
  0.0 0.8 copy.6.q_docs
  0.8 0.5 fusion
  1.4 0.1 pad_maximum_fusion
  1.5 0.0 copy-start.1
  1.5 1.0 copy-done.1
  2.6 0.0 copy-start.2
  2.6 1.0 copy-done.2
  3.6 0.0 copy-start.3
  3.6 0.7 copy-done.3
  4.3 0.0 copy-start
  4.3 97.0 %project.1 = (bf16[5,256,512]{2,1,0:T(8,128)(2,1)S(1)}, bf16[5,256,512]{2,1,0:T(8,128)(2,1)S(1)}, s32[5,1,256]{2,1,0:T(1,128)S(1)}) custom-call(bf16[256,8192]{1,0:T(8,128)(2,1)} %hidden.1, bf16[512,512]{1,0:T(8,128)(2,1)S(1)} %copy-done.1, bf16[512,512]{1,0:T(8,128)(2,1)S(1)} %copy-done.2, f32[256,128]{1,0:T(8,128)S(1)} %get-tuple-element.14.cos2, ...), custom_call_target="tpu_custom_call" | custom-call | tf_op jit(solution)/shard_map/project/pallas_call | solution.py:282
  101.3 0.0 copy-done
  101.3 26.3 %attend.1 = bf16[256,4096]{1,0:T(8,128)(2,1)} custom-call(bf16[256,4096]{1,0:T(8,128)(2,1)S(1)} %copy-done, bf16[1280,512]{1,0:T(8,128)(2,1)S(1)} %bitcast.5, bf16[1280,512]{1,0:T(8,128)(2,1)S(1)} %bitcast.6, s32[1,1280]{1,0:T(1,128)S(1)} %bitcast.7, s32[256,1]{1,0:T(8,128)S(1)} %copy.6.q_docs), custom_call_target="tpu_custom_call" | custom-call | tf_op jit(solution)/shard_map/attend/pallas_call | solution.py:303
  (2 shorter events, 0.0 us)
Async XLA Ops:
  1.5 1.0 copy-start.1
  2.6 1.0 copy-start.2
  3.6 0.7 copy-start.3
  4.3 97.0 %copy-start = (bf16[256,4096]{1,0:T(8,128)(2,1)S(1)}, bf16[256,4096]{1,0:T(8,128)(2,1)}, u32[]{:S(2)}) copy-start(bf16[256,4096]{1,0:T(8,128)(2,1)} %q.1) | copy-start | bytes 6291460

commit v2 on v1

v2 whole, which is shorter than its diff:
```python
import functools
import math

import jax
import jax.numpy as jnp
from jax import lax
from jax.experimental import pallas as pl
from jax.experimental.pallas import tpu as pltpu
from jax.sharding import PartitionSpec as P

HEAD_DIM = 128
HEADS = 32
KV_HEADS = 4
REACH = 4
GROUP = HEADS // KV_HEADS
MESH = pl.DeviceIdType.MESH


def fused_kernel(n, parts, hidden, queries, wk, wv, cos2, sin2, doc, out,
                 w_all, normed, q_all, probs, bias, acc, kbuf, vbuf, dbuf,
                 own_sem, ring_s, ring_r, sib_s, sib_r, x_s, x_r,
                 xs_s, xs_r, ex_s, ex_r, doc_s, doc_r):
    chips = n // 2
    rows = wk.shape[0]
    half = rows // 2
    third = (half // 48) * 16 if parts == 2 else 0
    length = half - third
    first = (length // 32) * 16
    subs = ((0, first), (first, length - first))
    tok, depth = hidden.shape
    blocks = REACH + 1
    span = blocks * tok

    idx = lax.axis_index("ctx")
    part = lax.axis_index("parts")
    core = idx % 2
    chip_no = idx // 2
    col = chip_no % 2
    lane = chip_no // 2
    pos = col * (chips - 1 - lane) + (1 - col) * lane
    sibling = idx + 1 - 2 * core

    def chip_at(place):
        upper = place // (chips // 2)
        return (1 - upper) * 2 * place + upper * (2 * (chips - 1 - place) + 1)

    def base(d, s, which_core):
        owner = (pos + chips - s) % chips if d == 0 else (pos + s) % chips
        return (2 * chip_at(owner) + which_core) * rows + d * half

    def at(m, start, count):
        return w_all.at[m, pl.ds(pl.multiple_of(start, 16), count), :]

    def ring(m, d, u, s, recv_s):
        target = (pos + 1) % chips if d == 0 else (pos + chips - 1) % chips
        piece = at(m, base(d, s, core) + part * third + subs[u][0], subs[u][1])
        return pltpu.make_async_remote_copy(
            piece, piece, ring_s.at[m, d, u, s], ring_r.at[m, d, u, recv_s],
            device_id={"ctx": 2 * chip_at(target) + core}, device_id_type=MESH)

    def sib_own(m, d, which_core):
        piece = at(m, base(d, 0, which_core), half)
        return pltpu.make_async_remote_copy(
            piece, piece, sib_s.at[m, d, 0], sib_r.at[m, d, 0],
            device_id={"ctx": sibling}, device_id_type=MESH)

    def sib(m, d, s, which_core):
        piece = at(m, base(d, s, which_core) + part * third, length)
        return pltpu.make_async_remote_copy(
            piece, piece, sib_s.at[m, d, s], sib_r.at[m, d, s],
            device_id={"ctx": sibling}, device_id_type=MESH)

    def cross(m, d, s, of_part):
        piece = at(m, base(d, s, core) + of_part * (half - third), third)
        return pltpu.make_async_remote_copy(
            piece, piece, x_s.at[m, d, s], x_r.at[m, d, s],
            device_id={"parts": 1 - part}, device_id_type=MESH)

    def cross_sib(m, d, s, which_core):
        piece = at(m, base(d, s, which_core) + (1 - part) * (half - third), third)
        return pltpu.make_async_remote_copy(
            piece, piece, xs_s.at[m, d, s], xs_r.at[m, d, s],
            device_id={"ctx": sibling}, device_id_type=MESH)

    def send_docs(o):
        return pltpu.make_async_remote_copy(
            doc, dbuf.at[o], doc_s.at[o - 1], doc_r.at[o - 1],
            device_id={"ctx": (idx + o) % n}, device_id_type=MESH)

    kvw = wk.shape[1]
    groups = ((kbuf, slice(0, kvw)), (vbuf, slice(0, kvw // 2)), (vbuf, slice(kvw // 2, kvw)))

    def send_ahead(e, o):
        buf, cols = groups[e]
        return pltpu.make_async_remote_copy(
            buf.at[0, :, cols], buf.at[o, :, cols], ex_s.at[e, o - 1], ex_r.at[e, o - 1],
            device_id={"ctx": (idx + o) % n}, device_id_type=MESH)

    def send_beside(e, o):
        buf, cols = groups[e]
        return pltpu.make_async_remote_copy(
            buf.at[o - 1 + 2 * core, :, cols], buf.at[o, :, cols], ex_s.at[e, o - 1],
            ex_r.at[e, o - 1], device_id={"ctx": sibling}, device_id_type=MESH)

    def pass_on(e):
        for o in (2, 4):
            @pl.when(idx + o < n)
            def _():
                send_ahead(e, o).start()

    def pass_beside(e):
        for o in (2, 4):
            @pl.when(idx >= o)
            def _():
                send_ahead(e, o).wait_recv()
        for o in (1, 3):
            @pl.when(sibling >= o)
            def _():
                send_beside(e, o).start()

    def passed(e):
        for o in (1, 3):
            @pl.when(idx >= o)
            def _():
                send_beside(e, o).wait_recv()

    own = [pltpu.make_async_copy(w, at(m, idx * rows, rows), own_sem.at[m])
           for m, w in ((0, wk), (1, wv))]
    own += [pltpu.make_async_copy(hidden, normed, own_sem.at[2]),
            pltpu.make_async_copy(queries, q_all, own_sem.at[3])]
    for copy in own:
        copy.start()

    barrier = pltpu.get_barrier_semaphore()
    greeted = [{"ctx": (idx + o) % n} for o in range(1, REACH + 1)]
    greeted += [{"ctx": (idx + n - o) % n} for o in range(1, REACH + 1)]
    greeted += [{"ctx": 2 * chip_at((pos + o) % chips) + core} for o in (1, chips - 1)]
    greeted += [{"ctx": sibling}]
    if third:
        greeted += [{"parts": 1 - part}]
    for who in greeted:
        pl.semaphore_signal(barrier, inc=1, device_id=who, device_id_type=MESH)
    pl.semaphore_wait(barrier, len(greeted))

    ways = (0, 1)

    def begin(m):
        for u in (0, 1):
            for d in ways:
                ring(m, d, u, 0, 1).start()
        for d in ways:
            sib_own(m, d, core).start()

    def turn(m, s):
        for u in (0, 1):
            for d in ways:
                ring(m, d, u, s, s).wait_recv()

                @pl.when(s < chips - 1)
                def _():
                    ring(m, d, u, s, s + 1).start()
        for d in ways:
            if third:
                cross(m, d, s, part).start()
            sib(m, d, s, core).start()
        if third:
            @pl.when(s > 1)
            def _():
                for d in ways:
                    cross(m, d, s - 1, 1 - part).wait_recv()
                    cross_sib(m, d, s - 1, core).start()

    def last_cross(m):
        if third:
            for d in ways:
                cross(m, d, chips - 1, 1 - part).wait_recv()
                cross_sib(m, d, chips - 1, core).start()

    def gathered(m):
        for d in ways:
            sib_own(m, d, 1 - core).wait_recv()

        @pl.loop(1, chips)
        def _(s):
            for d in ways:
                sib(m, d, s, 1 - core).wait_recv()
                if third:
                    cross_sib(m, d, s, 1 - core).wait_recv()

    def project(m, cols):
        step = 1024
        for i in range(depth // step):
            part_sum = jnp.dot(normed[:, i * step:(i + 1) * step],
                               w_all[m, i * step:(i + 1) * step, cols],
                               preferred_element_type=jnp.float32)
            acc[:, cols] = part_sum if i == 0 else acc[:, cols] + part_sum

    own[0].wait()
    begin(0)
    own[1].wait()
    for o in range(1, blocks):
        @pl.when(idx + o < n)
        def _():
            send_docs(o).start()

        @pl.when(idx < o)
        def _():
            kbuf[o] = jnp.zeros(kbuf.shape[1:], kbuf.dtype)
            vbuf[o] = jnp.zeros(vbuf.shape[1:], vbuf.dtype)
            dbuf[o] = jnp.full(dbuf.shape[1:], -1, dbuf.dtype)
    dbuf[0] = doc[...]
    own[2].wait()

    @pl.loop(0, tok // 16)
    def _(i):
        r16 = pl.ds(pl.multiple_of(i * 16, 16), 16)
        x = normed[r16, :].astype(jnp.float32)
        mean = jnp.sum(x * x, -1, keepdims=True) * (1.0 / depth)
        normed[r16, :] = (x * lax.rsqrt(mean + 1e-05)).astype(jnp.bfloat16)

    own[3].wait()

    @pl.loop(1, chips)
    def _(s):
        turn(0, s)

        @pl.when(s == chips - 2)
        def _():
            begin(1)

    for o in range(1, blocks):
        @pl.when(idx >= o)
        def _():
            send_docs(o).wait_recv()
    q_docs = jnp.transpose(jnp.broadcast_to(doc[...], (tok, tok)))
    for b in range(blocks):
        allowed = dbuf[b] == q_docs
        if b == 0:
            allowed &= (lax.broadcasted_iota(jnp.int32, (tok, tok), 1)
                        <= lax.broadcasted_iota(jnp.int32, (tok, tok), 0))
        bias[:, b * tok:(b + 1) * tok] = jnp.where(allowed, 0.0, -jnp.inf)

    last_cross(0)
    gathered(0)
    turn(1, 1)
    project(0, slice(0, kvw))
    for h in range(KV_HEADS):
        cols = slice(h * HEAD_DIM, (h + 1) * HEAD_DIM)
        x = acc[:, cols]
        turned = x * cos2[...] + pltpu.roll(x, HEAD_DIM // 2, 1) * sin2[...]
        kbuf[0, :, cols] = turned.astype(jnp.bfloat16)
    pass_on(0)
    turn(1, 2)
    pass_beside(0)
    turn(1, 3)
    passed(0)

    @pl.loop(4, chips - 4)
    def _(s):
        turn(1, s)

    scale = math.log2(math.e) / math.sqrt(HEAD_DIM)
    per_step = 2

    @pl.loop(0, HEADS // per_step)
    def _(i):
        @pl.when((i % 3 == 0) & (i < 12))
        def _():
            turn(1, chips - 4 + i // 3)

        @pl.when(i == 12)
        def _():
            last_cross(1)

        for g in range(per_step):
            h = i * per_step + g
            q = q_all[:, pl.ds(pl.multiple_of(h * HEAD_DIM, HEAD_DIM), HEAD_DIM)]
            k_cols = pl.ds(pl.multiple_of((h // GROUP) * HEAD_DIM, HEAD_DIM), HEAD_DIM)
            k = kbuf[:, :, k_cols].reshape(span, HEAD_DIM)
            scores = lax.dot_general(q, k, (((1,), (1,)), ((), ())),
                                     preferred_element_type=jnp.float32) + bias[...]
            top = jnp.max(scores, -1, keepdims=True)
            expo = jnp.exp2((scores - top) * scale)
            total = jnp.sum(expo, -1, keepdims=True)
            probs[h] = (expo * (1.0 / total)).astype(jnp.bfloat16)

    gathered(1)
    for e in (1, 2):
        cols = groups[e][1]
        project(1, cols)
        vbuf[0, :, cols] = acc[:, cols].astype(jnp.bfloat16)
        pass_on(e)
    pass_beside(1)
    pass_beside(2)
    for e in (1, 2):
        passed(e)

        @pl.loop((e - 1) * HEADS // 2 // per_step, e * HEADS // 2 // per_step)
        def _(i):
            for g in range(per_step):
                h = i * per_step + g
                v_cols = pl.ds(pl.multiple_of((h // GROUP) * HEAD_DIM, HEAD_DIM), HEAD_DIM)
                v = vbuf[:, :, v_cols].reshape(span, HEAD_DIM)
                out[:, pl.ds(pl.multiple_of(h * HEAD_DIM, HEAD_DIM), HEAD_DIM)] = jnp.dot(
                    probs[h], v, preferred_element_type=jnp.float32).astype(jnp.bfloat16)

    for e in range(3):
        for o in (1, 3):
            @pl.when(sibling >= o)
            def _():
                send_beside(e, o).wait_send()
        for o in (2, 4):
            @pl.when(idx + o < n)
            def _():
                send_ahead(e, o).wait_send()
    for o in range(1, blocks):
        @pl.when(idx + o < n)
        def _():
            send_docs(o).wait_send()

    for m in (0, 1):
        for d in ways:
            for u in (0, 1):
                ring(m, d, u, 0, 1).wait_send()
            sib_own(m, d, core).wait_send()

    @pl.loop(1, chips)
    def _(s):
        for m in (0, 1):
            for d in ways:
                @pl.when(s < chips - 1)
                def _():
                    for u in (0, 1):
                        ring(m, d, u, s, s).wait_send()

                sib(m, d, s, core).wait_send()
                if third:
                    cross(m, d, s, part).wait_send()
                    cross_sib(m, d, s, core).wait_send()


def on_device(n, parts, hidden_states, queries, w_key, w_value, doc_ids):
    tok, depth = hidden_states.shape
    kvw = w_key.shape[1]
    half_dim = HEAD_DIM // 2
    inverse_freq = 500000.0 ** (-jnp.arange(half_dim).astype(jnp.float32) * 2.0 / HEAD_DIM)
    positions = lax.axis_index("ctx") * tok + jnp.arange(tok)
    angles = positions.astype(jnp.float32)[:, None] * inverse_freq[None, :]
    cosine, sine = jnp.cos(angles), jnp.sin(angles)
    cos2 = jnp.concatenate([cosine, cosine], -1)
    sin2 = jnp.concatenate([-sine, sine], -1)
    chips = n // 2
    sem = pltpu.SemaphoreType.DMA
    blocks = REACH + 1
    in_vmem = pl.BlockSpec(memory_space=pltpu.VMEM)
    in_any = pl.BlockSpec(memory_space=pl.ANY)
    return pl.pallas_call(
        functools.partial(fused_kernel, n, parts),
        out_shape=jax.ShapeDtypeStruct(queries.shape, jnp.bfloat16),
        in_specs=[in_any, in_any, in_any, in_any, in_vmem, in_vmem, in_vmem],
        out_specs=in_vmem,
        scratch_shapes=[
            pltpu.VMEM((2, depth, kvw), jnp.bfloat16),
            pltpu.VMEM((tok, depth), jnp.bfloat16),
            pltpu.VMEM(queries.shape, jnp.bfloat16),
            pltpu.VMEM((HEADS, tok, blocks * tok), jnp.bfloat16),
            pltpu.VMEM((tok, blocks * tok), jnp.float32),
            pltpu.VMEM((tok, kvw), jnp.float32),
            pltpu.VMEM((blocks, tok, kvw), jnp.bfloat16),
            pltpu.VMEM((blocks, tok, kvw), jnp.bfloat16),
            pltpu.VMEM((blocks, 1, tok), jnp.int32),
            sem((4,)),
        ] + [sem((2, 2, 2, chips))] * 2 + [sem((2, 2, chips))] * 6
        + [sem((3, REACH))] * 2 + [sem((REACH,))] * 2,
        compiler_params=pltpu.CompilerParams(
            collective_id=0, has_side_effects=True, vmem_limit_bytes=60 * 2**20),
        name="project_attend",
    )(hidden_states, queries, w_key, w_value, cos2, sin2, doc_ids.reshape(1, tok))


def solution(mesh):
    in_specs = (
        P(("parts", "ctx"), None),
        P(("parts", "ctx"), None),
        P("ctx", None),
        P("ctx", None),
        P(("parts", "ctx")),
    )
    out_specs = P(("parts", "ctx"), None)
    return jax.shard_map(
        functools.partial(on_device, mesh.shape["ctx"], mesh.shape["parts"]),
        mesh=mesh, in_specs=in_specs, out_specs=out_specs, check_vma=False
    )
```

time: 129 us -> 122 us (0.946); the launches traced: 128 us -> 122 us
  Pallas kernels: 123 us -> 117 us
    pallas_call x2 -> x1, Pallas kernels: 123 us -> 117 us  [on_device(): pl.pallas_call(functools.partial(fused_kernel, n, parts), out_shape=jax.S...]
    unnamed x8 -> x1, local copies, waits for them, and re-layouts: 2.76 us -> 3.13 us
where the time goes in v2:
time: 122 us
  Pallas kernels  117 us (96%)
  local copies, waits for them, and re-layouts  3.13 us (3%)
  other arithmetic  1.4 us (1%)
    pallas_call x1, Pallas kernels, on_device(): pl.pallas_call(functools.partial(fused_kernel, n, parts), out_shape=jax.S...  117 us
    unnamed x1, local copies, waits for them, and re-layouts  3.13 us

profile of v2, /device:TPU:20, one launch (start us, length us, event | category | flops | bytes accessed | tf_op | source)
XLA Modules:
  0.0 122.0 jit_solution(8245979552731092400)
XLA Ops:
  0.0 0.5 fusion
  0.6 0.8 pad_maximum_fusion
  1.4 117.5 %project_attend.1 = bf16[256,4096]{1,0:T(8,128)(2,1)} custom-call(bf16[256,8192]{1,0:T(8,128)(2,1)} %hidden.1, bf16[256,4096]{1,0:T(8,128)(2,1)} %queries.1, bf16[512,512]{1,0:T(8,128)(2,1)} %wk.1, bf16[512,512]{1,0:T(8,128)(2,1)} %wv.1, f32[256,128]{1,0:T(8,128)} %get-tuple-element.8.cos2, f32[256,128]{1,0:T(8,128)} %get-tuple-element.9.sin2, s32[1,256]{1,0:T(1,128)} %bitcast.1), custom_call_target="tpu_custom_call" | custom-call | tf_op jit(solution)/shard_map/project_attend/pallas_call | solution.py:357
  118.9 3.1 %copy.7 = bf16[256,4096]{1,0:T(8,128)(2,1)} copy(bf16[256,4096]{1,0:T(8,128)(2,1)} %project_attend.1) | data formatting | bytes 4194304
  (2 shorter events, 0.0 us)

commit v3 on v2

--- a/solution.py
+++ b/solution.py
@@ -27,6 +27,7 @@
     length = half - third
     first = (length // 32) * 16
     subs = ((0, first), (first, length - first))
+    piecewise = half % 128 == 0
     tok, depth = hidden.shape
     blocks = REACH + 1
     span = blocks * tok
@@ -169,25 +170,58 @@
                 for d in ways:
                     cross(m, d, s - 1, 1 - part).wait_recv()
                     cross_sib(m, d, s - 1, core).start()
-
-    def last_cross(m):
-        if third:
-            for d in ways:
-                cross(m, d, chips - 1, 1 - part).wait_recv()
-                cross_sib(m, d, chips - 1, core).start()
-
-    def gathered(m):
-        for d in ways:
-            sib_own(m, d, 1 - core).wait_recv()
-
-        @pl.loop(1, chips)
-        def _(s):
+        if piecewise:
+            @pl.when(s > 1)
+            def _():
+                absorb(m, s - 2)
+
+    def absorb(m, s):
+        @pl.when(s == 0)
+        def _():
+            for d in ways:
+                sib_own(m, d, 1 - core).wait_recv()
+            acc[...] = jnp.zeros_like(acc)
+
+        @pl.when(s > 0)
+        def _():
             for d in ways:
                 sib(m, d, s, 1 - core).wait_recv()
                 if third:
                     cross_sib(m, d, s, 1 - core).wait_recv()
 
+        total = acc[...]
+        for d in ways:
+            for c in (0, 1):
+                start = base(d, s, c)
+                total += jnp.dot(
+                    normed[:, pl.ds(pl.multiple_of(start, 128), half)], at(m, start, half)[...],
+                    preferred_element_type=jnp.float32)
+        acc[...] = total
+
+    def last_cross(m):
+        if third:
+            for d in ways:
+                cross(m, d, chips - 1, 1 - part).wait_recv()
+                cross_sib(m, d, chips - 1, core).start()
+
+    def gathered(m):
+        if piecewise:
+            absorb(m, chips - 2)
+            absorb(m, chips - 1)
+            return
+        for d in ways:
+            sib_own(m, d, 1 - core).wait_recv()
+
+        @pl.loop(1, chips)
+        def _(s):
+            for d in ways:
+                sib(m, d, s, 1 - core).wait_recv()
+                if third:
+                    cross_sib(m, d, s, 1 - core).wait_recv()
+
     def project(m, cols):
+        if piecewise:
+            return
         step = 1024
         for i in range(depth // step):
             part_sum = jnp.dot(normed[:, i * step:(i + 1) * step],
@@ -343,12 +377,12 @@
     tok, depth = hidden_states.shape
     kvw = w_key.shape[1]
     half_dim = HEAD_DIM // 2
-    inverse_freq = 500000.0 ** (-jnp.arange(half_dim).astype(jnp.float32) * 2.0 / HEAD_DIM)
+    place = jnp.arange(HEAD_DIM)
+    inverse_freq = 500000.0 ** (-(place % half_dim).astype(jnp.float32) * 2.0 / HEAD_DIM)
     positions = lax.axis_index("ctx") * tok + jnp.arange(tok)
     angles = positions.astype(jnp.float32)[:, None] * inverse_freq[None, :]
-    cosine, sine = jnp.cos(angles), jnp.sin(angles)
-    cos2 = jnp.concatenate([cosine, cosine], -1)
-    sin2 = jnp.concatenate([-sine, sine], -1)
+    cos2 = jnp.cos(angles)
+    sin2 = jnp.sin(angles) * jnp.where(place < half_dim, -1.0, 1.0)[None, :]
     chips = n // 2
     sem = pltpu.SemaphoreType.DMA
     blocks = REACH + 1

time: 122 us -> 121 us (level)
    mul x0 -> x1, other arithmetic: none -> 1.25 us  [on_device(): sin2 = jnp.sin(angles) * jnp.where(place < half_dim, -1.0, 1.0)[None, :]]
where the time goes in v3:
time: 121 us
  Pallas kernels  116 us (96%)
  local copies, waits for them, and re-layouts  3.13 us (3%)
  other arithmetic  1.26 us (1%)
    pallas_call x1, Pallas kernels, on_device(): pl.pallas_call(functools.partial(fused_kernel, n, parts), out_shape=jax.S...  116 us
    unnamed x1, local copies, waits for them, and re-layouts  3.13 us

profile of v3, /device:TPU:20, one launch (start us, length us, event | category | flops | bytes accessed | tf_op | source)
XLA Modules:
  0.0 120.8 jit_solution(1516206014202960021)
XLA Ops:
  0.0 1.2 %fusion = (f32[256,128]{1,0:T(8,128)}, f32[256,128]{1,0:T(8,128)}) fusion(f32[128]{0:T(128)S(1)} %get-tuple-element.7, f32[128]{0:T(128)S(1)} %get-tuple-element.8, f32[256]{0:T(256)S(1)} %add_convert_fusion), kind=kLoop, calls=%fused_computation.2 | loop fusion | flops 65536 | bytes 264192 | tf_op jit(solution)/shard_map/mul | solution.py:385
  1.3 116.4 %project_attend.1 = bf16[256,4096]{1,0:T(8,128)(2,1)} custom-call(bf16[256,8192]{1,0:T(8,128)(2,1)} %hidden.1, bf16[256,4096]{1,0:T(8,128)(2,1)} %queries.1, bf16[512,512]{1,0:T(8,128)(2,1)} %wk.1, bf16[512,512]{1,0:T(8,128)(2,1)} %wv.1, f32[256,128]{1,0:T(8,128)} %get-tuple-element.6.cos2, f32[256,128]{1,0:T(8,128)} %get-tuple-element.5.sin2, s32[1,256]{1,0:T(1,128)} %bitcast.1), custom_call_target="tpu_custom_call" | custom-call | tf_op jit(solution)/shard_map/project_attend/pallas_call | solution.py:391
  117.7 3.1 %copy.7 = bf16[256,4096]{1,0:T(8,128)(2,1)} copy(bf16[256,4096]{1,0:T(8,128)(2,1)} %project_attend.1) | data formatting | bytes 4194304
  (2 shorter events, 0.0 us)

commit v4 on v3

--- a/solution.py
+++ b/solution.py
@@ -180,7 +180,7 @@
         def _():
             for d in ways:
                 sib_own(m, d, 1 - core).wait_recv()
-            acc[...] = jnp.zeros_like(acc)
+            acc[m] = jnp.zeros(acc.shape[1:], acc.dtype)
 
         @pl.when(s > 0)
         def _():
@@ -189,14 +189,14 @@
                 if third:
                     cross_sib(m, d, s, 1 - core).wait_recv()
 
-        total = acc[...]
+        total = acc[m]
         for d in ways:
             for c in (0, 1):
                 start = base(d, s, c)
                 total += jnp.dot(
                     normed[:, pl.ds(pl.multiple_of(start, 128), half)], at(m, start, half)[...],
                     preferred_element_type=jnp.float32)
-        acc[...] = total
+        acc[m] = total
 
     def last_cross(m):
         if third:
@@ -227,7 +227,7 @@
             part_sum = jnp.dot(normed[:, i * step:(i + 1) * step],
                                w_all[m, i * step:(i + 1) * step, cols],
                                preferred_element_type=jnp.float32)
-            acc[:, cols] = part_sum if i == 0 else acc[:, cols] + part_sum
+            acc[m, :, cols] = part_sum if i == 0 else acc[m, :, cols] + part_sum
 
     own[0].wait()
     begin(0)
@@ -258,9 +258,13 @@
     def _(s):
         turn(0, s)
 
-        @pl.when(s == chips - 2)
+        @pl.when(s == chips - 4)
         def _():
             begin(1)
+
+        @pl.when(s > chips - 4)
+        def _():
+            turn(1, s - (chips - 4))
 
     for o in range(1, blocks):
         @pl.when(idx >= o)
@@ -276,20 +280,19 @@
 
     last_cross(0)
     gathered(0)
-    turn(1, 1)
     project(0, slice(0, kvw))
     for h in range(KV_HEADS):
         cols = slice(h * HEAD_DIM, (h + 1) * HEAD_DIM)
-        x = acc[:, cols]
+        x = acc[0, :, cols]
         turned = x * cos2[...] + pltpu.roll(x, HEAD_DIM // 2, 1) * sin2[...]
         kbuf[0, :, cols] = turned.astype(jnp.bfloat16)
     pass_on(0)
-    turn(1, 2)
+    turn(1, 4)
     pass_beside(0)
-    turn(1, 3)
+    turn(1, 5)
     passed(0)
 
-    @pl.loop(4, chips - 4)
+    @pl.loop(6, chips - 2)
     def _(s):
         turn(1, s)
 
@@ -298,13 +301,27 @@
 
     @pl.loop(0, HEADS // per_step)
     def _(i):
-        @pl.when((i % 3 == 0) & (i < 12))
-        def _():
-            turn(1, chips - 4 + i // 3)
-
-        @pl.when(i == 12)
+        @pl.when((i % 3 == 0) & (i < 6))
+        def _():
+            turn(1, chips - 2 + i // 3)
+
+        @pl.when(i == 6)
         def _():
             last_cross(1)
+
+        @pl.when(i == 9)
+        def _():
+            gathered(1)
+            for e in (1, 2):
+                cols = groups[e][1]
+                project(1, cols)
+                vbuf[0, :, cols] = acc[1, :, cols].astype(jnp.bfloat16)
+                pass_on(e)
+
+        @pl.when(i == 14)
+        def _():
+            pass_beside(1)
+            pass_beside(2)
 
         for g in range(per_step):
             h = i * per_step + g
@@ -318,14 +335,6 @@
             total = jnp.sum(expo, -1, keepdims=True)
             probs[h] = (expo * (1.0 / total)).astype(jnp.bfloat16)
 
-    gathered(1)
-    for e in (1, 2):
-        cols = groups[e][1]
-        project(1, cols)
-        vbuf[0, :, cols] = acc[:, cols].astype(jnp.bfloat16)
-        pass_on(e)
-    pass_beside(1)
-    pass_beside(2)
     for e in (1, 2):
         passed(e)
 
@@ -399,7 +408,7 @@
             pltpu.VMEM(queries.shape, jnp.bfloat16),
             pltpu.VMEM((HEADS, tok, blocks * tok), jnp.bfloat16),
             pltpu.VMEM((tok, blocks * tok), jnp.float32),
-            pltpu.VMEM((tok, kvw), jnp.float32),
+            pltpu.VMEM((2, tok, kvw), jnp.float32),
             pltpu.VMEM((blocks, tok, kvw), jnp.bfloat16),
             pltpu.VMEM((blocks, tok, kvw), jnp.bfloat16),
             pltpu.VMEM((blocks, 1, tok), jnp.int32),

time: 121 us -> 119 us (0.983)
  Pallas kernels: 116 us -> 114 us
    pallas_call x1, Pallas kernels: 116 us -> 114 us  [on_device(): pl.pallas_call(functools.partial(fused_kernel, n, parts), out_shape=jax.S...]
where the time goes in v4:
time: 119 us; the launch traced here: 118 us
  Pallas kernels  114 us (96%)
  local copies, waits for them, and re-layouts  3.13 us (3%)
  other arithmetic  1.26 us (1%)
    pallas_call x1, Pallas kernels, on_device(): pl.pallas_call(functools.partial(fused_kernel, n, parts), out_shape=jax.S...  114 us
    unnamed x1, local copies, waits for them, and re-layouts  3.13 us

profile of v4, /device:TPU:20, one launch (start us, length us, event | category | flops | bytes accessed | tf_op | source)
XLA Modules:
  0.0 118.5 jit_solution(11524726727832865708)
XLA Ops:
  0.0 1.2 %fusion = (f32[256,128]{1,0:T(8,128)}, f32[256,128]{1,0:T(8,128)}) fusion(f32[128]{0:T(128)S(1)} %get-tuple-element.7, f32[128]{0:T(128)S(1)} %get-tuple-element.8, f32[256]{0:T(256)S(1)} %add_convert_fusion), kind=kLoop, calls=%fused_computation.2 | loop fusion | flops 65536 | bytes 264192 | tf_op jit(solution)/shard_map/mul | solution.py:394
  1.3 114.1 %project_attend.1 = bf16[256,4096]{1,0:T(8,128)(2,1)} custom-call(bf16[256,8192]{1,0:T(8,128)(2,1)} %hidden.1, bf16[256,4096]{1,0:T(8,128)(2,1)} %queries.1, bf16[512,512]{1,0:T(8,128)(2,1)} %wk.1, bf16[512,512]{1,0:T(8,128)(2,1)} %wv.1, f32[256,128]{1,0:T(8,128)} %get-tuple-element.6.cos2, f32[256,128]{1,0:T(8,128)} %get-tuple-element.5.sin2, s32[1,256]{1,0:T(1,128)} %bitcast.1), custom_call_target="tpu_custom_call" | custom-call | tf_op jit(solution)/shard_map/project_attend/pallas_call | solution.py:400
  115.3 3.1 %copy.7 = bf16[256,4096]{1,0:T(8,128)(2,1)} copy(bf16[256,4096]{1,0:T(8,128)(2,1)} %project_attend.1) | data formatting | bytes 4194304
  (2 shorter events, 0.0 us)
